TPU v7x, 32 devices: a whole 2x2x4 slice. The times are simulated.
32 devices in a mesh: groups: 2 (over y), hist: 4 (over z), tower: 2 (over x), head: 2 (over core).
Axes of the slice: x: 2, y: 2, z: 4, core: 2. Of those that a mesh axis runs over, the one named last changes fastest.
Arguments:
- queries: bfloat16 [1024, 1024], P(('groups', 'hist', 'tower'), 'head'), parts along dimension 0, may hold values from -6 to 6
- hist_keys: bfloat16 [4, 1024, 1024], P('groups', 'hist', 'head'), parts along dimension 0, may hold values from -6 to 6
- hist_values: bfloat16 [4, 1024, 1024], P('groups', 'hist', 'head'), parts along dimension 0, may hold values from -6 to 6
- cand_user: int32 [1024], P(('groups', 'hist', 'tower')), parts along dimension 0, may hold values from 0 to 1
- time_bucket: int32 [4, 1024], P('groups', 'hist'), parts along dimension 0, may hold values from 0 to 127
- hist_len: int32 [4], P('groups'), parts along dimension 0, may hold values from 256 to 1024
- cand_gate: bfloat16 [1024, 1024], P(('groups', 'hist', 'tower'), 'head'), parts along dimension 0, may hold values from -6 to 6
- time_bias: float32 [128, 8], P(None, 'head'), may hold values from -4 to 4
- tower_in: bfloat16 [1024, 4096], P('head', 'tower'), may hold values from -0.1875 to 0.1875
- tower_bias: float32 [4096], P('tower'), may hold values from -4 to 4
- tower_out: float32 [4096], P('tower'), may hold values from -0.09375 to 0.09375
Outputs:
- cand_states: bfloat16 [1024, 1024], P(('groups', 'hist', 'tower'), 'head'), parts along dimension 0
- cand_scores: float32 [1024], P(('groups', 'hist', 'tower')), parts along dimension 0
There are 2 independent parts, one for each index of `groups`. A program takes and returns all parts, laid end to end along the dimension named above; an argument that names none is the same for every part. Nothing has to cross between parts.
All inputs are finite; a program needn't handle non-finite values.
Results may differ from a plain program's by a relative error of at most 0.017.
Values may be sent and summed in bfloat16 or wider, within the bound.
No kernel may reach another device: no remote copies, remote signals or barrier semaphores. Data moves between devices by JAX's collectives and lax.ppermute only.
A program may use at most 64 MiB of HBM per device.

v0:
```python
import functools

import jax
import jax.numpy as jnp
from jax import lax
from jax.experimental import pallas as pl
from jax.experimental.pallas import tpu as pltpu
from jax.sharding import PartitionSpec as P

DH = 128
LANES = 128
DEAD = -1e30
HBM = pl.BlockSpec(memory_space=pltpu.HBM)
VMEM = pl.BlockSpec(memory_space=pltpu.VMEM)
SMEM = pl.BlockSpec(memory_space=pltpu.SMEM)
LIMIT = 32 * 1024 * 1024
BIASCOST = 1000000000
SHARECOST = 16


def GROUPS(remote):
    return [remote[-1:], remote[:-1]]


def partner(index, step, count):
    if count & (count - 1) == 0:
        return index ^ step
    return (index + step) % count


def fetch(x, axis, step, count):
    return lax.ppermute(x, axis, [(partner(i, step, count), i) for i in range(count)])


def give(x, axis, step, count):
    return lax.ppermute(x, axis, [(i, partner(i, step, count)) for i in range(count)])


def call(body, outs, specs, flops, nbytes, out_specs=None, scratch=(), limit=LIMIT):
    return pl.pallas_call(
        body,
        out_shape=outs,
        in_specs=specs,
        out_specs=out_specs or jax.tree.map(lambda _: VMEM, outs),
        scratch_shapes=scratch,
        compiler_params=pltpu.CompilerParams(vmem_limit_bytes=limit),
        cost_estimate=pl.CostEstimate(
            flops=flops, bytes_accessed=nbytes, transcendentals=0
        ),
    )


def bias_body(len_ref, bucket_ref, table_ref, out_ref):
    users, events = bucket_ref.shape
    heads, buckets = table_ref.shape
    table = table_ref[...] * 0.5
    high = table.astype(jnp.bfloat16)
    rest = table - high.astype(jnp.float32)
    middle = rest.astype(jnp.bfloat16)
    low = (rest - middle.astype(jnp.float32)).astype(jnp.bfloat16)
    position = lax.axis_index("hist") * events + lax.broadcasted_iota(
        jnp.int32, (heads, events), 1
    )
    bucket_ids = lax.broadcasted_iota(jnp.int32, (buckets, events), 0)
    for user in range(users):
        onehot = jnp.where(bucket_ids == bucket_ref[user : user + 1, :], 1.0, 0.0).astype(
            jnp.bfloat16
        )
        bias = sum(
            jnp.dot(piece, onehot, preferred_element_type=jnp.float32)
            for piece in (high, middle, low)
        )
        out_ref[user * heads : (user + 1) * heads, :] = jnp.where(
            position < len_ref[user], bias, DEAD
        )


def share_body(blocks, *refs):
    packed_refs, (k_ref, v_ref, bias_ref), out_refs = (
        refs[:blocks],
        refs[blocks : blocks + 3],
        refs[blocks + 3 :],
    )
    users, events, width = k_ref.shape
    each = out_refs[0].shape[0]
    heads = width // DH
    half_scale = 0.5 * DH ** (-0.5)
    ones = jnp.ones((8, LANES), jnp.bfloat16)
    owner = jnp.concatenate(
        [
            lax.dot_general(
                ref[each:, :LANES],
                ones,
                (((0,), (0,)), ((), ())),
                preferred_element_type=jnp.float32,
            )[:each]
            for ref in packed_refs
        ],
        axis=0,
    )
    mine = [owner == float(user) for user in range(users)]
    wide = [
        jnp.concatenate([owner] * (events // LANES), axis=1) == float(user)
        for user in range(users)
    ]
    for head in range(heads):
        cols = slice(head * DH, (head + 1) * DH)
        query = jnp.concatenate([ref[:each, cols] for ref in packed_refs], axis=0)
        query = query.astype(jnp.float32)
        query = jnp.concatenate(
            [jnp.where(mask, query, 0.0).astype(jnp.bfloat16) for mask in mine], axis=1
        )
        keys = jnp.concatenate([k_ref[user, :, cols] for user in range(users)], axis=1)
        logits = lax.dot_general(
            query, keys, (((1,), (1,)), ((), ())), preferred_element_type=jnp.float32
        )
        bias = jnp.broadcast_to(bias_ref[head : head + 1, :], logits.shape)
        for user in range(1, users):
            row = user * heads + head
            bias = jnp.where(wide[user], bias_ref[row : row + 1, :], bias)
        half = logits * half_scale + bias
        weight = (half * jnp.tanh(half) + half).astype(jnp.bfloat16)
        values = jnp.concatenate([v_ref[user, :, cols] for user in range(users)], axis=1)
        mixed = jnp.dot(weight, values, preferred_element_type=jnp.float32)
        share = mixed[:, :DH]
        for user in range(1, users):
            share = jnp.where(mine[user], mixed[:, user * DH : (user + 1) * DH], share)
        share = share.astype(jnp.bfloat16)
        for block, out_ref in enumerate(out_refs):
            out_ref[:, cols] = share[block * each : (block + 1) * each]


def total_body(*refs):
    *share_refs, total_ref, sent_ref = refs
    total = share_refs[0][...].astype(jnp.float32)
    for share_ref in share_refs[1:]:
        total = total + share_ref[...].astype(jnp.float32)
    total_ref[...] = total
    sent_ref[...] = total.astype(jnp.bfloat16)


def tower_body(blocks, sides, *refs):
    parts = blocks * sides
    rows_refs, gate_refs, refs = refs[:parts], refs[parts : 2 * parts], refs[2 * parts :]
    weight_refs = refs[:sides]
    bias_ref, out_w_ref = refs[sides], refs[sides + 1]
    states_ref, *score_refs, own_buf, sem = refs[sides + 2 :]
    count = own_buf.shape[0]
    features = sides * own_buf.shape[1]
    states = [[] for _ in range(sides)]
    for b in range(blocks):
        rows = [rows_refs[side * blocks + b][...].astype(jnp.float32) for side in range(sides)]
        row_sum = sum(jnp.sum(x, axis=1, keepdims=True) for x in rows)
        row_squares = sum(jnp.sum(x * x, axis=1, keepdims=True) for x in rows)
        mean = row_sum / features
        variance = row_squares / features - mean * mean
        scale = lax.rsqrt(variance + 1e-05)
        for side in range(sides):
            gate = gate_refs[side * blocks + b][...].astype(jnp.float32)
            states[side].append(((rows[side] - mean) * scale * gate).astype(jnp.bfloat16))
        if b == 0:
            own_buf[...] = states[0][0]
            keep = pltpu.make_async_copy(own_buf, states_ref, sem)
            keep.start()
    states = [jnp.concatenate(x, axis=0) for x in states]
    units = weight_refs[0].shape[1]
    step = min(256, units)
    total = jnp.zeros((count * blocks, LANES), jnp.float32)
    for first in range(0, units, step):
        cols = slice(first, first + step)
        act = bias_ref[:, cols]
        for side in range(sides):
            act = act + jnp.dot(
                states[side], weight_refs[side][:, cols], preferred_element_type=jnp.float32
            )
        half = 0.5 * act
        hidden = half * jnp.tanh(half) + half
        part = hidden * out_w_ref[:, cols]
        for lane in range(0, step, LANES):
            total = total + part[:, lane : lane + LANES]
    scores = jnp.sum(total.T, axis=0, keepdims=True)
    for b in range(blocks):
        score_refs[b][...] = scores[:, b * count : (b + 1) * count]
    keep.wait()


def local(
    sizes,
    queries,
    hist_keys,
    hist_values,
    cand_user,
    time_bucket,
    hist_len,
    cand_gate,
    time_bias,
    tower_in,
    tower_bias,
    tower_out,
):
    hists, towers, sides = sizes["hist"], sizes["tower"], sizes["head"]
    users, events, width = hist_keys.shape
    count = queries.shape[0]
    heads = width // DH
    features = width * sides
    f32, bf16 = jnp.float32, jnp.bfloat16

    owners = jnp.pad(cand_user.astype(bf16).reshape(1, count), ((0, 7), (0, width - count)))
    packed = jnp.concatenate([queries, owners], axis=0)
    blocks = [packed] + [fetch(packed, "hist", step, hists) for step in range(1, hists)]

    share_type = jax.ShapeDtypeStruct((count, width), bf16)
    bias = call(
        bias_body,
        jax.ShapeDtypeStruct((users * heads, events), f32),
        [SMEM, VMEM, VMEM],
        BIASCOST,
        users * heads * events * 4,
    )(hist_len, time_bucket, time_bias.T)

    def shares_of(group):
        return call(
            functools.partial(share_body, len(group)),
            [share_type] * len(group),
            [VMEM] * (len(group) + 3),
            SHARECOST * len(group) * count * users * events * width,
            4 * users * events * width,
        )(*group, hist_keys, hist_values, bias)

    shares = list(shares_of([packed]))
    remote = [(step, blocks[step]) for step in range(1, hists)]
    for group in GROUPS(remote):
        for (step, _), share in zip(group, shares_of([block for _, block in group])):
            shares.append(give(share, "hist", step, hists))

    total, sent = call(
        total_body,
        (jax.ShapeDtypeStruct((count, width), f32), share_type),
        [VMEM] * hists,
        8 * count * width,
        8 * count * width,
    )(*shares)

    def spread(x):
        near = [x] + [fetch(x, "tower", step, towers) for step in range(1, towers)]
        far = [fetch(y, "head", step, sides) for step in range(1, sides) for y in near]
        return near + far

    gates = spread(cand_gate)
    weights = [tower_in] + [fetch(tower_in, "head", step, sides) for step in range(1, sides)]
    rows = spread(sent)
    rows[0] = total
    units = tower_in.shape[1]
    cand_states, *scores = call(
        functools.partial(tower_body, towers, sides),
        (share_type,) + tuple(jax.ShapeDtypeStruct((1, count), f32) for _ in range(towers)),
        [VMEM] * (2 * towers * sides + sides + 2),
        2 * towers * count * features * units,
        2 * features * units,
        out_specs=(pl.BlockSpec(memory_space=pl.ANY),) + (VMEM,) * towers,
        scratch=[pltpu.VMEM((count, width), bf16), pltpu.SemaphoreType.DMA],
    )(*rows, *gates, *weights, tower_bias.reshape(1, -1), tower_out.reshape(1, -1))
    cand_scores = scores[0]
    for step in range(1, towers):
        cand_scores = cand_scores + give(scores[step], "tower", step, towers)
    return (cand_states, cand_scores.reshape(count))


def solution(mesh):
    return jax.shard_map(
        functools.partial(local, dict(mesh.shape)),
        mesh=mesh,
        in_specs=(
            P(("groups", "hist", "tower"), "head"),
            P("groups", "hist", "head"),
            P("groups", "hist", "head"),
            P(("groups", "hist", "tower")),
            P("groups", "hist"),
            P("groups"),
            P(("groups", "hist", "tower"), "head"),
            P(None, "head"),
            P("head", "tower"),
            P("tower"),
            P("tower"),
        ),
        out_specs=(P(("groups", "hist", "tower"), "head"), P(("groups", "hist", "tower"))),
        check_vma=False,
    )
```

profile of v0, /device:TPU:0, one launch (start us, length us, event | category | flops | bytes accessed | tf_op | source)
XLA Modules:
  0.0 34.9 jit_solution(16525043248901078781)
XLA Ops:
  0.7 0.5 %collective-permute-start.12 = (bf16[512,2048]{1,0:T(8,128)(2,1)}, bf16[512,2048]{1,0:T(8,128)(2,1)S(1)}, u32[]{:S(2)}, u32[]{:S(2)}) collective-permute-start(bf16[512,2048]{1,0:T(8,128)(2,1)} %refs_8_.1), channel_id=1, source_target_pairs={{1,0},{0,1},{3,2},{2,3},{5,4},{4,5},{7,6},{6,7},{9,8},{8,9},{11,10... | collective-permute-start | bytes 6291464 | tf_op jit(solution)/shard_map/ppermute | solution.py:32
  1.2 0.7 %convert_bitcast_fusion = bf16[1,64]{1,0:T(2,128)(2,1)S(1)} fusion(s32[64]{0:T(128)} %param.14), kind=kLoop, calls=%fused_computation.4 | loop fusion | flops 64 | bytes 384 | tf_op jit(solution)/shard_map/reshape | solution.py:208
  1.8 0.8 %fusion.1.refs_0_ = bf16[72,512]{1,0:T(8,128)(2,1)S(1)} fusion(bf16[1,64]{1,0:T(2,128)(2,1)S(1)} %convert_bitcast_fusion, bf16[64,512]{1,0:T(8,128)(2,1)} %param.11), kind=kLoop, calls=%fused_computation.2 | loop fusion | flops 221184 | bytes 139392 | tf_op jit(solution)/shard_map/concatenate | solution.py:209
  2.7 3.7 %collective-permute-start.3 = (bf16[72,512]{1,0:T(8,128)(2,1)S(1)}, bf16[72,512]{1,0:T(8,128)(2,1)S(1)}, u32[]{:S(2)}, u32[]{:S(2)}) collective-permute-start(bf16[72,512]{1,0:T(8,128)(2,1)S(1)} %fusion.1.refs_0_), channel_id=1, source_target_pairs={{8,0},{12,4},{0,8},{4,12},{9,1},{13,5},{1,9},{5,13},{10,2},{14,6},... | collective-permute-start | bytes 221192 | tf_op jit(solution)/shard_map/ppermute | solution.py:32
  6.3 1.6 %collective-permute-start.2 = (bf16[72,512]{1,0:T(8,128)(2,1)S(1)}, bf16[72,512]{1,0:T(8,128)(2,1)S(1)}, u32[]{:S(2)}, u32[]{:S(2)}) collective-permute-start(bf16[72,512]{1,0:T(8,128)(2,1)S(1)} %fusion.1.refs_0_), channel_id=1, source_target_pairs={{4,0},{0,4},{12,8},{8,12},{5,1},{1,5},{13,9},{9,13},{6,2},{2,6},{1... | collective-permute-start | bytes 221192 | tf_op jit(solution)/shard_map/ppermute | solution.py:32
  7.9 0.7 %copy-done.6 = s32[2,256]{1,0:T(2,128)S(1)} copy-done((s32[2,256]{1,0:T(2,128)S(1)}, s32[2,256]{1,0:T(2,128)}, u32[]{:S(2)}) %copy-start.6) | copy-done | bytes 2072
  8.6 0.7 %copy-done.7 = f32[128,4]{0,1:T(4,128)S(1)} copy-done((f32[128,4]{0,1:T(4,128)S(1)}, f32[128,4]{0,1:T(4,128)}, u32[]{:S(2)}) %copy-start.7) | copy-done | bytes 2072
  9.3 0.7 %copy-done.8 = s32[2]{0:T(128)S(1)} copy-done((s32[2]{0:T(128)S(1)}, s32[2]{0:T(128)}, u32[]{:S(2)}) %copy-start.8) | copy-done | bytes 32
  9.9 0.7 %shard_map.122.refs_3_.refs_4_ = f32[8,256]{1,0:T(8,128)S(1)} custom-call(s32[2]{0:T(128)S(1)} %copy-done.8, s32[2,256]{1,0:T(2,128)S(1)} %copy-done.6, f32[4,128]{1,0:T(4,128)S(1)} %bitcast.9), custom_call_target="tpu_custom_call" | custom-call | flops 1000000000 | bytes 8192 | tf_op jit(solution)/shard_map/pallas_call | solution.py:213
  11.1 1.0 %shard_map.125 = (bf16[64,512]{1,0:T(8,128)(2,1)S(1)}, bf16[64,512]{1,0:T(8,128)(2,1)S(1)}) custom-call(bf16[72,512]{1,0:T(8,128)(2,1)S(1)} %collective-permute-done.2.refs_0_, bf16[72,512]{1,0:T(8,128)(2,1)S(1)} %collective-permute-done.3.refs_1_, bf16[2,256,512]{2,1,0:T(8,128)(2,1)S(1)} %copy-done.1, bf16[2,256,512]{2,1,0:T(8,128)(2,1)S(1)} %copy-done.2, ...), custom_call_target="tpu_custom_call" | custom-call | flops 536870912 | bytes 1048576 | tf_op jit(solution)/shard_map/pallas_call | solution.py:222
  12.2 2.0 %collective-permute-start.4 = (bf16[64,512]{1,0:T(8,128)(2,1)S(1)}, bf16[64,512]{1,0:T(8,128)(2,1)S(1)}, u32[]{:S(2)}, u32[]{:S(2)}) collective-permute-start(bf16[64,512]{1,0:T(8,128)(2,1)S(1)} %get-tuple-element.9), channel_id=1, source_target_pairs={{0,4},{4,0},{8,12},{12,8},{1,5},{5,1},{9,13},{13,9},{2,6},{6,2},{1... | collective-permute-start | bytes 196616 | tf_op jit(solution)/shard_map/ppermute | solution.py:36
  14.2 2.4 %collective-permute-start.5 = (bf16[64,512]{1,0:T(8,128)(2,1)S(1)}, bf16[64,512]{1,0:T(8,128)(2,1)S(1)}, u32[]{:S(2)}, u32[]{:S(2)}) collective-permute-start(bf16[64,512]{1,0:T(8,128)(2,1)S(1)} %get-tuple-element.10), channel_id=1, source_target_pairs={{0,8},{4,12},{8,0},{12,4},{1,9},{5,13},{9,1},{13,5},{2,10},{6,14},... | collective-permute-start | bytes 196616 | tf_op jit(solution)/shard_map/ppermute | solution.py:36
  16.6 1.0 %shard_map.124 = bf16[64,512]{1,0:T(8,128)(2,1)S(1)} custom-call(bf16[72,512]{1,0:T(8,128)(2,1)S(1)} %collective-permute-done.refs_0_, bf16[2,256,512]{2,1,0:T(8,128)(2,1)S(1)} %copy-done.1, bf16[2,256,512]{2,1,0:T(8,128)(2,1)S(1)} %copy-done.2, f32[8,256]{1,0:T(8,128)S(1)} %shard_map.122.refs_3_.refs_4_), custom_call_target="tpu_custom_call" | custom-call | flops 268435456 | bytes 1048576 | tf_op jit(solution)/shard_map/pallas_call | solution.py:222
  17.7 1.6 %collective-permute-start.9 = (bf16[64,512]{1,0:T(8,128)(2,1)S(1)}, bf16[64,512]{1,0:T(8,128)(2,1)S(1)}, u32[]{:S(2)}, u32[]{:S(2)}) collective-permute-start(bf16[64,512]{1,0:T(8,128)(2,1)S(1)} %copy-done.3), channel_id=1, source_target_pairs={{2,0},{0,2},{3,1},{1,3},{6,4},{4,6},{7,5},{5,7},{10,8},{8,10},{11,... | collective-permute-start | bytes 196616 | tf_op jit(solution)/shard_map/ppermute | solution.py:32
  19.3 1.0 %shard_map.123.refs_0_ = bf16[64,512]{1,0:T(8,128)(2,1)S(1)} custom-call(bf16[72,512]{1,0:T(8,128)(2,1)S(1)} %fusion.1.refs_0_, bf16[2,256,512]{2,1,0:T(8,128)(2,1)S(1)} %copy-done.1, bf16[2,256,512]{2,1,0:T(8,128)(2,1)S(1)} %copy-done.2, f32[8,256]{1,0:T(8,128)S(1)} %shard_map.122.refs_3_.refs_4_), custom_call_target="tpu_custom_call" | custom-call | flops 268435456 | bytes 1048576 | tf_op jit(solution)/shard_map/pallas_call | solution.py:222
  20.7 3.0 %collective-permute-done.1.refs_1_ = bf16[64,512]{1,0:T(8,128)(2,1)S(1)} collective-permute-done((bf16[64,512]{1,0:T(8,128)(2,1)S(1)}, bf16[64,512]{1,0:T(8,128)(2,1)S(1)}, u32[]{:S(2)}, u32[]{:S(2)}) %collective-permute-start.1) | collective-permute-done | bytes 65568 | tf_op jit(solution)/shard_map/ppermute | solution.py:36
  23.8 1.6 %collective-permute-start.6 = (bf16[64,512]{1,0:T(8,128)(2,1)S(1)}, bf16[64,512]{1,0:T(8,128)(2,1)S(1)}, u32[]{:S(2)}, u32[]{:S(2)}) collective-permute-start(bf16[64,512]{1,0:T(8,128)(2,1)S(1)} %get-tuple-element.12), channel_id=1, source_target_pairs={{2,0},{0,2},{3,1},{1,3},{6,4},{4,6},{7,5},{5,7},{10,8},{8,10},{11,... | collective-permute-start | bytes 196616 | tf_op jit(solution)/shard_map/ppermute | solution.py:32
  25.3 0.5 %collective-permute-start.11 = (bf16[64,512]{1,0:T(8,128)(2,1)S(1)}, bf16[64,512]{1,0:T(8,128)(2,1)S(1)}, u32[]{:S(2)}, u32[]{:S(2)}) collective-permute-start(bf16[64,512]{1,0:T(8,128)(2,1)S(1)} %collective-permute-done.9.refs_5_), channel_id=1, source_target_pairs={{1,0},{0,1},{3,2},{2,3},{5,4},{4,5},{7,6},{6,7},{9,8},{8,9},{11,10... | collective-permute-start | bytes 196616 | tf_op jit(solution)/shard_map/ppermute | solution.py:32
  25.9 2.3 %collective-permute-done.6.refs_1_ = bf16[64,512]{1,0:T(8,128)(2,1)S(1)} collective-permute-done((bf16[64,512]{1,0:T(8,128)(2,1)S(1)}, bf16[64,512]{1,0:T(8,128)(2,1)S(1)}, u32[]{:S(2)}, u32[]{:S(2)}) %collective-permute-start.6) | collective-permute-done | bytes 65568 | tf_op jit(solution)/shard_map/ppermute | solution.py:32
  28.1 1.2 %collective-permute-done.8.refs_3_ = bf16[64,512]{1,0:T(8,128)(2,1)S(1)} collective-permute-done((bf16[64,512]{1,0:T(8,128)(2,1)S(1)}, bf16[64,512]{1,0:T(8,128)(2,1)S(1)}, u32[]{:S(2)}, u32[]{:S(2)}) %collective-permute-start.8) | collective-permute-done | bytes 65568 | tf_op jit(solution)/shard_map/ppermute | solution.py:32
  29.4 1.4 %shard_map.127 = (bf16[64,512]{1,0:T(8,128)(2,1)}, f32[1,64]{1,0:T(1,128)S(1)}, f32[1,64]{1,0:T(1,128)S(1)}) custom-call(f32[64,512]{1,0:T(8,128)S(1)} %get-tuple-element.11.refs_0_, bf16[64,512]{1,0:T(8,128)(2,1)S(1)} %collective-permute-done.6.refs_1_, bf16[64,512]{1,0:T(8,128)(2,1)S(1)} %collective-permute-done.7.refs_2_, ...), custom_call_target="tpu_custom_call" | custom-call | flops 536870912 | bytes 4194304 | tf_op jit(solution)/shard_map/pallas_call | solution.py:254
  30.8 1.6 %collective-permute-start.13 = (f32[1,64]{1,0:T(1,128)S(1)}, f32[1,64]{1,0:T(1,128)S(1)}, u32[]{:S(2)}, u32[]{:S(2)}) collective-permute-start(f32[1,64]{1,0:T(1,128)S(1)} %get-tuple-element.15), channel_id=1, source_target_pairs={{0,2},{2,0},{1,3},{3,1},{4,6},{6,4},{5,7},{7,5},{8,10},{10,8},{9,1... | collective-permute-start | bytes 776 | tf_op jit(solution)/shard_map/ppermute | solution.py:36
  32.3 2.1 %collective-permute-done.13 = f32[1,64]{1,0:T(1,128)S(1)} collective-permute-done((f32[1,64]{1,0:T(1,128)S(1)}, f32[1,64]{1,0:T(1,128)S(1)}, u32[]{:S(2)}, u32[]{:S(2)}) %collective-permute-start.13) | collective-permute-done | bytes 288 | tf_op jit(solution)/shard_map/ppermute | solution.py:36
  34.4 0.5 %add_bitcast_fusion = f32[64]{0:T(128)} fusion(f32[1,64]{1,0:T(1,128)S(1)} %get-tuple-element.14, f32[1,64]{1,0:T(1,128)S(1)} %collective-permute-done.13), kind=kLoop, calls=%fused_computation.3 | loop fusion | flops 64 | bytes 768 | tf_op jit(solution)/shard_map/reshape | solution.py:266
  (31 shorter events, 1.1 us)
Async XLA Ops:
  0.6 10.5 %copy-start.2 = (bf16[2,256,512]{2,1,0:T(8,128)(2,1)S(1)}, bf16[2,256,512]{2,1,0:T(8,128)(2,1)}, u32[]{:S(2)}) copy-start(bf16[2,256,512]{2,1,0:T(8,128)(2,1)} %refs_3_.1) | copy-start | bytes 1572868
  0.6 10.5 %copy-start.1 = (bf16[2,256,512]{2,1,0:T(8,128)(2,1)S(1)}, bf16[2,256,512]{2,1,0:T(8,128)(2,1)}, u32[]{:S(2)}) copy-start(bf16[2,256,512]{2,1,0:T(8,128)(2,1)} %refs_2_.5) | copy-start | bytes 1572868
  0.7 28.7 %collective-permute-start.12 = (bf16[512,2048]{1,0:T(8,128)(2,1)}, bf16[512,2048]{1,0:T(8,128)(2,1)S(1)}, u32[]{:S(2)}, u32[]{:S(2)}) collective-permute-start(bf16[512,2048]{1,0:T(8,128)(2,1)} %refs_8_.1), channel_id=1, source_target_pairs={{1,0},{0,1},{3,2},{2,3},{5,4},{4,5},{7,6},{6,7},{9,8},{8,9},{11,10... | collective-permute-start | bytes 6291464 | tf_op jit(solution)/shard_map/ppermute | solution.py:32
  2.7 8.3 %collective-permute-start.3 = (bf16[72,512]{1,0:T(8,128)(2,1)S(1)}, bf16[72,512]{1,0:T(8,128)(2,1)S(1)}, u32[]{:S(2)}, u32[]{:S(2)}) collective-permute-start(bf16[72,512]{1,0:T(8,128)(2,1)S(1)} %fusion.1.refs_0_), channel_id=1, source_target_pairs={{8,0},{12,4},{0,8},{4,12},{9,1},{13,5},{1,9},{5,13},{10,2},{14,6},... | collective-permute-start | bytes 221192 | tf_op jit(solution)/shard_map/ppermute | solution.py:32
  6.3 4.8 %collective-permute-start.2 = (bf16[72,512]{1,0:T(8,128)(2,1)S(1)}, bf16[72,512]{1,0:T(8,128)(2,1)S(1)}, u32[]{:S(2)}, u32[]{:S(2)}) collective-permute-start(bf16[72,512]{1,0:T(8,128)(2,1)S(1)} %fusion.1.refs_0_), channel_id=1, source_target_pairs={{4,0},{0,4},{12,8},{8,12},{5,1},{1,5},{13,9},{9,13},{6,2},{2,6},{1... | collective-permute-start | bytes 221192 | tf_op jit(solution)/shard_map/ppermute | solution.py:32
  7.9 8.7 %collective-permute-start = (bf16[72,512]{1,0:T(8,128)(2,1)S(1)}, bf16[72,512]{1,0:T(8,128)(2,1)S(1)}, u32[]{:S(2)}, u32[]{:S(2)}) collective-permute-start(bf16[72,512]{1,0:T(8,128)(2,1)S(1)} %fusion.1.refs_0_), channel_id=1, source_target_pairs={{12,0},{8,4},{4,8},{0,12},{13,1},{9,5},{5,9},{1,13},{14,2},{10,6},... | collective-permute-start | bytes 221192 | tf_op jit(solution)/shard_map/ppermute | solution.py:32
  7.9 0.7 %copy-start.6 = (s32[2,256]{1,0:T(2,128)S(1)}, s32[2,256]{1,0:T(2,128)}, u32[]{:S(2)}) copy-start(s32[2,256]{1,0:T(2,128)} %bucket_ref.1) | copy-start | bytes 6148
  8.6 0.7 %copy-start.7 = (f32[128,4]{0,1:T(4,128)S(1)}, f32[128,4]{0,1:T(4,128)}, u32[]{:S(2)}) copy-start(f32[128,4]{0,1:T(4,128)} %param.18) | copy-start | bytes 6148
  9.3 0.7 %copy-start.8 = (s32[2]{0:T(128)S(1)}, s32[2]{0:T(128)}, u32[]{:S(2)}) copy-start(s32[2]{0:T(128)} %len_ref.1) | copy-start | bytes 28
  10.6 7.1 %copy-start.3 = (bf16[64,512]{1,0:T(8,128)(2,1)S(1)}, bf16[64,512]{1,0:T(8,128)(2,1)}, u32[]{:S(2)}) copy-start(bf16[64,512]{1,0:T(8,128)(2,1)} %refs_4_.1) | copy-start | bytes 196612
  10.7 18.7 %copy-start = (bf16[512,2048]{1,0:T(8,128)(2,1)S(1)}, bf16[512,2048]{1,0:T(8,128)(2,1)}, u32[]{:S(2)}) copy-start(bf16[512,2048]{1,0:T(8,128)(2,1)} %refs_8_.1) | copy-start | bytes 6291460
  10.7 18.7 %copy-start.4 = (f32[2048]{0:T(1024)S(1)}, f32[2048]{0:T(1024)}, u32[]{:S(2)}) copy-start(f32[2048]{0:T(1024)} %param.20) | copy-start | bytes 24580
  10.7 18.7 %copy-start.5 = (f32[2048]{0:T(1024)S(1)}, f32[2048]{0:T(1024)}, u32[]{:S(2)}) copy-start(f32[2048]{0:T(1024)} %param.21) | copy-start | bytes 24580
  12.2 8.1 %collective-permute-start.4 = (bf16[64,512]{1,0:T(8,128)(2,1)S(1)}, bf16[64,512]{1,0:T(8,128)(2,1)S(1)}, u32[]{:S(2)}, u32[]{:S(2)}) collective-permute-start(bf16[64,512]{1,0:T(8,128)(2,1)S(1)} %get-tuple-element.9), channel_id=1, source_target_pairs={{0,4},{4,0},{8,12},{12,8},{1,5},{5,1},{9,13},{13,9},{2,6},{6,2},{1... | collective-permute-start | bytes 196616 | tf_op jit(solution)/shard_map/ppermute | solution.py:36
  14.2 6.6 %collective-permute-start.5 = (bf16[64,512]{1,0:T(8,128)(2,1)S(1)}, bf16[64,512]{1,0:T(8,128)(2,1)S(1)}, u32[]{:S(2)}, u32[]{:S(2)}) collective-permute-start(bf16[64,512]{1,0:T(8,128)(2,1)S(1)} %get-tuple-element.10), channel_id=1, source_target_pairs={{0,8},{4,12},{8,0},{12,4},{1,9},{5,13},{9,1},{13,5},{2,10},{6,14},... | collective-permute-start | bytes 196616 | tf_op jit(solution)/shard_map/ppermute | solution.py:36
  17.6 6.1 %collective-permute-start.1 = (bf16[64,512]{1,0:T(8,128)(2,1)S(1)}, bf16[64,512]{1,0:T(8,128)(2,1)S(1)}, u32[]{:S(2)}, u32[]{:S(2)}) collective-permute-start(bf16[64,512]{1,0:T(8,128)(2,1)S(1)} %shard_map.124), channel_id=1, source_target_pairs={{0,12},{4,8},{8,4},{12,0},{1,13},{5,9},{9,5},{13,1},{2,14},{6,10},... | collective-permute-start | bytes 196616 | tf_op jit(solution)/shard_map/ppermute | solution.py:36
  17.7 7.6 %collective-permute-start.9 = (bf16[64,512]{1,0:T(8,128)(2,1)S(1)}, bf16[64,512]{1,0:T(8,128)(2,1)S(1)}, u32[]{:S(2)}, u32[]{:S(2)}) collective-permute-start(bf16[64,512]{1,0:T(8,128)(2,1)S(1)} %copy-done.3), channel_id=1, source_target_pairs={{2,0},{0,2},{3,1},{1,3},{6,4},{4,6},{7,5},{5,7},{10,8},{8,10},{11,... | collective-permute-start | bytes 196616 | tf_op jit(solution)/shard_map/ppermute | solution.py:32
  23.8 4.3 %collective-permute-start.6 = (bf16[64,512]{1,0:T(8,128)(2,1)S(1)}, bf16[64,512]{1,0:T(8,128)(2,1)S(1)}, u32[]{:S(2)}, u32[]{:S(2)}) collective-permute-start(bf16[64,512]{1,0:T(8,128)(2,1)S(1)} %get-tuple-element.12), channel_id=1, source_target_pairs={{2,0},{0,2},{3,1},{1,3},{6,4},{4,6},{7,5},{5,7},{10,8},{8,10},{11,... | collective-permute-start | bytes 196616 | tf_op jit(solution)/shard_map/ppermute | solution.py:32
  25.3 2.8 %collective-permute-start.10 = (bf16[64,512]{1,0:T(8,128)(2,1)S(1)}, bf16[64,512]{1,0:T(8,128)(2,1)S(1)}, u32[]{:S(2)}, u32[]{:S(2)}) collective-permute-start(bf16[64,512]{1,0:T(8,128)(2,1)S(1)} %copy-done.3), channel_id=1, source_target_pairs={{1,0},{0,1},{3,2},{2,3},{5,4},{4,5},{7,6},{6,7},{9,8},{8,9},{11,10... | collective-permute-start | bytes 196616 | tf_op jit(solution)/shard_map/ppermute | solution.py:32
  25.3 2.8 %collective-permute-start.11 = (bf16[64,512]{1,0:T(8,128)(2,1)S(1)}, bf16[64,512]{1,0:T(8,128)(2,1)S(1)}, u32[]{:S(2)}, u32[]{:S(2)}) collective-permute-start(bf16[64,512]{1,0:T(8,128)(2,1)S(1)} %collective-permute-done.9.refs_5_), channel_id=1, source_target_pairs={{1,0},{0,1},{3,2},{2,3},{5,4},{4,5},{7,6},{6,7},{9,8},{8,9},{11,10... | collective-permute-start | bytes 196616 | tf_op jit(solution)/shard_map/ppermute | solution.py:32
  25.8 2.3 %collective-permute-start.7 = (bf16[64,512]{1,0:T(8,128)(2,1)S(1)}, bf16[64,512]{1,0:T(8,128)(2,1)S(1)}, u32[]{:S(2)}, u32[]{:S(2)}) collective-permute-start(bf16[64,512]{1,0:T(8,128)(2,1)S(1)} %get-tuple-element.12), channel_id=1, source_target_pairs={{1,0},{0,1},{3,2},{2,3},{5,4},{4,5},{7,6},{6,7},{9,8},{8,9},{11,10... | collective-permute-start | bytes 196616 | tf_op jit(solution)/shard_map/ppermute | solution.py:32
  28.1 1.3 %collective-permute-start.8 = (bf16[64,512]{1,0:T(8,128)(2,1)S(1)}, bf16[64,512]{1,0:T(8,128)(2,1)S(1)}, u32[]{:S(2)}, u32[]{:S(2)}) collective-permute-start(bf16[64,512]{1,0:T(8,128)(2,1)S(1)} %collective-permute-done.6.refs_1_), channel_id=1, source_target_pairs={{1,0},{0,1},{3,2},{2,3},{5,4},{4,5},{7,6},{6,7},{9,8},{8,9},{11,10... | collective-permute-start | bytes 196616 | tf_op jit(solution)/shard_map/ppermute | solution.py:32
  30.8 3.6 %collective-permute-start.13 = (f32[1,64]{1,0:T(1,128)S(1)}, f32[1,64]{1,0:T(1,128)S(1)}, u32[]{:S(2)}, u32[]{:S(2)}) collective-permute-start(f32[1,64]{1,0:T(1,128)S(1)} %get-tuple-element.15), channel_id=1, source_target_pairs={{0,2},{2,0},{1,3},{3,1},{4,6},{6,4},{5,7},{7,5},{8,10},{10,8},{9,1... | collective-permute-start | bytes 776 | tf_op jit(solution)/shard_map/ppermute | solution.py:36
where the time goes:
time: 35.1 us; the launch traced here: 34.9 us
  starting transfers between devices  15.5 us (44%)
  waiting for transfers between devices  9.42 us (27%)
  Pallas kernels  5.18 us (15%)
  local copies, waits for them, and re-layouts  2.04 us (6%)
  other arithmetic  2.02 us (6%)
  between operations  0.75 us (2%)
    ppermute x10, starting transfers between devices, fetch(): lax.ppermute(x, axis, [(partner(i, step, count), i) for i in range(count)])  9.4 us
    ppermute x4, starting transfers between devices, give(): lax.ppermute(x, axis, [(i, partner(i, step, count)) for i in range(count)])  6.07 us
    ppermute x4, waiting for transfers between devices, give(): lax.ppermute(x, axis, [(i, partner(i, step, count)) for i in range(count)])  5.49 us
    ppermute x10, waiting for transfers between devices, fetch(): lax.ppermute(x, axis, [(partner(i, step, count), i) for i in range(count)])  3.92 us
    pallas_call x3, Pallas kernels, shares_of(): call(functools.partial(share_body, len(group)), [share_type] * len(group)...  3.08 us
    unnamed x18, local copies, waits for them, and re-layouts  2.04 us
    pallas_call x1, Pallas kernels, local(): call(functools.partial(tower_body, towers, sides), (share_type,) + tuple(...  1.36 us
    concatenate x1, other arithmetic, local(): packed = jnp.concatenate([queries, owners], axis=0)  0.85 us
  transfers between devices with their start and end apart: 14, of which 7 were waited for; matrix products, arithmetic and copies ran while one was open for 4% of the time, Pallas kernels for 11%

commit v1 on v0

--- a/solution.py
+++ b/solution.py
@@ -14,12 +14,6 @@
 VMEM = pl.BlockSpec(memory_space=pltpu.VMEM)
 SMEM = pl.BlockSpec(memory_space=pltpu.SMEM)
 LIMIT = 32 * 1024 * 1024
-BIASCOST = 1000000000
-SHARECOST = 16
-
-
-def GROUPS(remote):
-    return [remote[-1:], remote[:-1]]
 
 
 def partner(index, step, count):
@@ -34,6 +28,10 @@
 
 def give(x, axis, step, count):
     return lax.ppermute(x, axis, [(i, partner(i, step, count)) for i in range(count)])
+
+
+def hbm(x):
+    return pltpu.with_memory_space_constraint(x, pltpu.HBM)
 
 
 def call(body, outs, specs, flops, nbytes, out_specs=None, scratch=(), limit=LIMIT):
@@ -50,7 +48,7 @@
     )
 
 
-def bias_body(len_ref, bucket_ref, table_ref, out_ref):
+def event_bias(len_ref, bucket_ref, table_ref, out_ref):
     users, events = bucket_ref.shape
     heads, buckets = table_ref.shape
     table = table_ref[...] * 0.5
@@ -75,6 +73,46 @@
         )
 
 
+def pack_body(q_ref, id_ref, out_ref, id_buf, sems):
+    count, width = q_ref.shape
+    copies = [
+        pltpu.make_async_copy(id_ref, id_buf, sems.at[0]),
+        pltpu.make_async_copy(q_ref, out_ref.at[pl.ds(0, count)], sems.at[1]),
+    ]
+    for copy in copies:
+        copy.start()
+    copies[0].wait()
+    ids = id_buf[...].astype(jnp.float32)
+    ids = jnp.concatenate([ids] * (width // count), axis=1)
+    out_ref[count:, :] = jnp.broadcast_to(ids, (out_ref.shape[0] - count, width)).astype(
+        jnp.bfloat16
+    )
+    copies[1].wait()
+
+
+def own_body(
+    packed_ref, k_ref, v_ref, bucket_ref, table_ref, len_ref,
+    share_ref, bias_ref, k_out, v_out,
+    bucket_buf, table_buf, len_buf, sems,
+):
+    pairs = [
+        (bucket_ref, bucket_buf),
+        (table_ref, table_buf),
+        (len_ref, len_buf),
+        (k_ref, k_out),
+        (v_ref, v_out),
+    ]
+    copies = [pltpu.make_async_copy(a, b, sems.at[i]) for i, (a, b) in enumerate(pairs)]
+    for copy in copies:
+        copy.start()
+    for copy in copies[:3]:
+        copy.wait()
+    event_bias(len_buf, bucket_buf, table_buf, bias_ref)
+    for copy in copies[3:]:
+        copy.wait()
+    share_body(1, packed_ref, k_out, v_out, bias_ref, share_ref)
+
+
 def share_body(blocks, *refs):
     packed_refs, (k_ref, v_ref, bias_ref), out_refs = (
         refs[:blocks],
@@ -85,12 +123,12 @@
     each = out_refs[0].shape[0]
     heads = width // DH
     half_scale = 0.5 * DH ** (-0.5)
-    ones = jnp.ones((8, LANES), jnp.bfloat16)
+    eighth = jnp.full((8, LANES), 0.125, jnp.bfloat16)
     owner = jnp.concatenate(
         [
             lax.dot_general(
                 ref[each:, :LANES],
-                ones,
+                eighth,
                 (((0,), (0,)), ((), ())),
                 preferred_element_type=jnp.float32,
             )[:each]
@@ -99,29 +137,34 @@
         axis=0,
     )
     mine = [owner == float(user) for user in range(users)]
+    half_mine = [owner.astype(jnp.bfloat16) == float(user) for user in range(users)]
     wide = [
         jnp.concatenate([owner] * (events // LANES), axis=1) == float(user)
         for user in range(users)
     ]
+    columns = [slice(head * DH, (head + 1) * DH) for head in range(heads)]
+    logits, weights = [], []
+    for cols in columns:
+        query = jnp.concatenate([ref[:each, cols] for ref in packed_refs], axis=0)
+        query = jnp.concatenate(
+            [jnp.where(mask, query, jnp.zeros_like(query)) for mask in half_mine], axis=1
+        )
+        keys = jnp.concatenate([k_ref[user, :, cols] for user in range(users)], axis=1)
+        logits.append(
+            lax.dot_general(
+                query, keys, (((1,), (1,)), ((), ())), preferred_element_type=jnp.float32
+            )
+        )
     for head in range(heads):
-        cols = slice(head * DH, (head + 1) * DH)
-        query = jnp.concatenate([ref[:each, cols] for ref in packed_refs], axis=0)
-        query = query.astype(jnp.float32)
-        query = jnp.concatenate(
-            [jnp.where(mask, query, 0.0).astype(jnp.bfloat16) for mask in mine], axis=1
-        )
-        keys = jnp.concatenate([k_ref[user, :, cols] for user in range(users)], axis=1)
-        logits = lax.dot_general(
-            query, keys, (((1,), (1,)), ((), ())), preferred_element_type=jnp.float32
-        )
-        bias = jnp.broadcast_to(bias_ref[head : head + 1, :], logits.shape)
+        bias = jnp.broadcast_to(bias_ref[head : head + 1, :], logits[head].shape)
         for user in range(1, users):
             row = user * heads + head
             bias = jnp.where(wide[user], bias_ref[row : row + 1, :], bias)
-        half = logits * half_scale + bias
-        weight = (half * jnp.tanh(half) + half).astype(jnp.bfloat16)
+        half = logits[head] * half_scale + bias
+        weights.append((half * jnp.tanh(half) + half).astype(jnp.bfloat16))
+    for head, cols in enumerate(columns):
         values = jnp.concatenate([v_ref[user, :, cols] for user in range(users)], axis=1)
-        mixed = jnp.dot(weight, values, preferred_element_type=jnp.float32)
+        mixed = jnp.dot(weights[head], values, preferred_element_type=jnp.float32)
         share = mixed[:, :DH]
         for user in range(1, users):
             share = jnp.where(mine[user], mixed[:, user * DH : (user + 1) * DH], share)
@@ -205,37 +248,53 @@
     features = width * sides
     f32, bf16 = jnp.float32, jnp.bfloat16
 
-    owners = jnp.pad(cand_user.astype(bf16).reshape(1, count), ((0, 7), (0, width - count)))
-    packed = jnp.concatenate([queries, owners], axis=0)
+    packed = call(
+        pack_body,
+        pltpu.VMEM((count + 8, width), bf16),
+        [HBM] * 2,
+        0,
+        4 * count * width,
+        scratch=[pltpu.VMEM((1, count), jnp.int32), pltpu.SemaphoreType.DMA((2,))],
+    )(hbm(queries), hbm(cand_user.reshape(1, count)))
     blocks = [packed] + [fetch(packed, "hist", step, hists) for step in range(1, hists)]
 
-    share_type = jax.ShapeDtypeStruct((count, width), bf16)
-    bias = call(
-        bias_body,
-        jax.ShapeDtypeStruct((users * heads, events), f32),
-        [SMEM, VMEM, VMEM],
-        BIASCOST,
-        users * heads * events * 4,
-    )(hist_len, time_bucket, time_bias.T)
+    share_type = pltpu.VMEM((count, width), bf16)
+    own_share, bias, keys, values = call(
+        own_body,
+        (
+            share_type,
+            pltpu.VMEM((users * heads, events), f32),
+            pltpu.VMEM(hist_keys.shape, bf16),
+            pltpu.VMEM(hist_values.shape, bf16),
+        ),
+        [VMEM] + [HBM] * 5,
+        0,
+        4 * users * events * width,
+        scratch=[
+            pltpu.VMEM(time_bucket.shape, jnp.int32),
+            pltpu.VMEM((heads, time_bias.shape[0]), f32),
+            pltpu.SMEM(hist_len.shape, jnp.int32),
+            pltpu.SemaphoreType.DMA((5,)),
+        ],
+    )(packed, *map(hbm, (hist_keys, hist_values, time_bucket, time_bias.T, hist_len)))
 
     def shares_of(group):
         return call(
             functools.partial(share_body, len(group)),
             [share_type] * len(group),
             [VMEM] * (len(group) + 3),
-            SHARECOST * len(group) * count * users * events * width,
+            0,
             4 * users * events * width,
-        )(*group, hist_keys, hist_values, bias)
-
-    shares = list(shares_of([packed]))
-    remote = [(step, blocks[step]) for step in range(1, hists)]
-    for group in GROUPS(remote):
-        for (step, _), share in zip(group, shares_of([block for _, block in group])):
-            shares.append(give(share, "hist", step, hists))
+        )(*group, keys, values, bias)
+
+    shares = [own_share]
+    for step in range(1, hists):
+        (share,) = shares_of([blocks[step]])
+        shares.append(give(share, "hist", step, hists))
 
     total, sent = call(
         total_body,
-        (jax.ShapeDtypeStruct((count, width), f32), share_type),
+        (pltpu.VMEM((count, width), f32), share_type),
         [VMEM] * hists,
         8 * count * width,
         8 * count * width,
@@ -246,6 +305,7 @@
         far = [fetch(y, "head", step, sides) for step in range(1, sides) for y in near]
         return near + far
 
+    cand_gate, _ = lax.optimization_barrier((cand_gate, shares[-1]))
     gates = spread(cand_gate)
     weights = [tower_in] + [fetch(tower_in, "head", step, sides) for step in range(1, sides)]
     rows = spread(sent)
@@ -253,7 +313,8 @@
     units = tower_in.shape[1]
     cand_states, *scores = call(
         functools.partial(tower_body, towers, sides),
-        (share_type,) + tuple(jax.ShapeDtypeStruct((1, count), f32) for _ in range(towers)),
+        (jax.ShapeDtypeStruct((count, width), bf16),)
+        + tuple(pltpu.VMEM((1, count), f32) for _ in range(towers)),
         [VMEM] * (2 * towers * sides + sides + 2),
         2 * towers * count * features * units,
         2 * features * units,

time: 35.1 us -> 31.9 us (0.909)
  local copies, waits for them, and re-layouts: 2.04 us -> 0.02 us
  other arithmetic: 2.02 us -> 0.51 us
  Pallas kernels: 5.18 us -> 5.7 us
    unnamed x18 -> x8, local copies, waits for them, and re-layouts: 2.04 us -> 0.02 us
    pallas_call x3 -> x4, Pallas kernels: 2.1 us -> 4.11 us  [the longest x1 1.84 us: local(): call(own_body, (share_type, pltpu.VMEM((users * heads, events), f32), plt...]
    pallas_call x3, Pallas kernels: 3.08 us -> 1.59 us  [shares_of(): call(functools.partial(share_body, len(group)), [share_type] * len(group)...]
    concatenate x1 -> x0, other arithmetic: 0.85 us -> none  [local(): packed = jnp.concatenate([queries, owners], axis=0)]
    reshape x1 -> x0, other arithmetic: 0.66 us -> none  [local(): cand_user.astype(bf16).reshape(1, count)]
    ppermute x4, waiting for transfers between devices: 5.49 us -> 5.01 us  [give(): lax.ppermute(x, axis, [(i, partner(i, step, count)) for i in range(count)])]
  transfers between devices with their start and end apart: 14 -> 14, of which waited for: 7 -> 7; matrix products, arithmetic and copies ran while one was open for 4% -> 0% of each run, Pallas kernels for 11% -> 14%
where the time goes in v1:
time: 31.9 us; the launch traced here: 31.7 us
  starting transfers between devices  15.6 us (49%)
  waiting for transfers between devices  9.15 us (29%)
  Pallas kernels  5.7 us (18%)
  between operations  0.74 us (2%)
  other arithmetic  0.51 us (2%)
    ppermute x10, starting transfers between devices, fetch(): lax.ppermute(x, axis, [(partner(i, step, count), i) for i in range(count)])  9.38 us
    ppermute x4, starting transfers between devices, give(): lax.ppermute(x, axis, [(i, partner(i, step, count)) for i in range(count)])  6.18 us
    ppermute x4, waiting for transfers between devices, give(): lax.ppermute(x, axis, [(i, partner(i, step, count)) for i in range(count)])  5.01 us
    ppermute x10, waiting for transfers between devices, fetch(): lax.ppermute(x, axis, [(partner(i, step, count), i) for i in range(count)])  4.14 us
    pallas_call x1, Pallas kernels, local(): call(own_body, (share_type, pltpu.VMEM((users * heads, events), f32), plt...  1.84 us
    pallas_call x3, Pallas kernels, shares_of(): call(functools.partial(share_body, len(group)), [share_type] * len(group)...  1.59 us
    pallas_call x1, Pallas kernels, local(): call(functools.partial(tower_body, towers, sides), (jax.ShapeDtypeStruct(...  1.36 us
    pallas_call x1, Pallas kernels, local(): call(pack_body, pltpu.VMEM((count + 8, width), bf16), [HBM] * 2, 0, 4 * c...  0.87 us
  transfers between devices with their start and end apart: 14, of which 7 were waited for; matrix products, arithmetic and copies ran while one was open for 0% of the time, Pallas kernels for 14%

profile of v1, /device:TPU:0, one launch (start us, length us, event | category | flops | bytes accessed | tf_op | source)
XLA Modules:
  0.0 31.7 jit_solution(15480898450061058229)
XLA Ops:
  0.6 0.5 %collective-permute-start.12 = (bf16[512,2048]{1,0:T(8,128)(2,1)}, bf16[512,2048]{1,0:T(8,128)(2,1)S(1)}, u32[]{:S(2)}, u32[]{:S(2)}) collective-permute-start(bf16[512,2048]{1,0:T(8,128)(2,1)} %refs_8_.1), channel_id=1, source_target_pairs={{1,0},{0,1},{3,2},{2,3},{5,4},{4,5},{7,6},{6,7},{9,8},{8,9},{11,10... | collective-permute-start | bytes 6291464 | tf_op jit(solution)/shard_map/ppermute | solution.py:26
  1.1 0.9 %shard_map.122.packed_ref = bf16[72,512]{1,0:T(8,128)(2,1)S(1)} custom-call(bf16[64,512]{1,0:T(8,128)(2,1)} %q_ref.1, s32[1,64]{1,0:T(1,128)} %bitcast.9), custom_call_target="tpu_custom_call" | custom-call | bytes 131072 | tf_op jit(solution)/shard_map/pallas_call | solution.py:251
  2.0 4.7 %collective-permute-start.4 = (bf16[72,512]{1,0:T(8,128)(2,1)S(1)}, bf16[72,512]{1,0:T(8,128)(2,1)S(1)}, u32[]{:S(2)}, u32[]{:S(2)}) collective-permute-start(bf16[72,512]{1,0:T(8,128)(2,1)S(1)} %shard_map.122.packed_ref), channel_id=1, source_target_pairs={{12,0},{8,4},{4,8},{0,12},{13,1},{9,5},{5,9},{1,13},{14,2},{10,6},... | collective-permute-start | bytes 221192 | tf_op jit(solution)/shard_map/ppermute | solution.py:26
  6.7 0.6 %collective-permute-start.2 = (bf16[72,512]{1,0:T(8,128)(2,1)S(1)}, bf16[72,512]{1,0:T(8,128)(2,1)S(1)}, u32[]{:S(2)}, u32[]{:S(2)}) collective-permute-start(bf16[72,512]{1,0:T(8,128)(2,1)S(1)} %shard_map.122.packed_ref), channel_id=1, source_target_pairs={{8,0},{12,4},{0,8},{4,12},{9,1},{13,5},{1,9},{5,13},{10,2},{14,6},... | collective-permute-start | bytes 221192 | tf_op jit(solution)/shard_map/ppermute | solution.py:26
  7.4 1.8 %shard_map.123 = (bf16[64,512]{1,0:T(8,128)(2,1)S(1)}, f32[8,256]{1,0:T(8,128)S(1)}, bf16[2,256,512]{2,1,0:T(8,128)(2,1)S(1)}, bf16[2,256,512]{2,1,0:T(8,128)(2,1)S(1)}) custom-call(bf16[72,512]{1,0:T(8,128)(2,1)S(1)} %shard_map.122.packed_ref, bf16[2,256,512]{2,1,0:T(8,128)(2,1)} %k_ref.1, bf16[2,256,512]{2,1,0:T(8,128)(2,1)} %v_ref.1, ...), custom_call_target="tpu_custom_call" | custom-call | bytes 1048576 | tf_op jit(solution)/shard_map/pallas_call | solution.py:262
  9.2 0.6 %collective-permute-done.4.refs_0_ = bf16[72,512]{1,0:T(8,128)(2,1)S(1)} collective-permute-done((bf16[72,512]{1,0:T(8,128)(2,1)S(1)}, bf16[72,512]{1,0:T(8,128)(2,1)S(1)}, u32[]{:S(2)}, u32[]{:S(2)}) %collective-permute-start.4) | collective-permute-done | bytes 73760 | tf_op jit(solution)/shard_map/ppermute | solution.py:26
  9.9 0.5 %shard_map.126 = bf16[64,512]{1,0:T(8,128)(2,1)S(1)} custom-call(bf16[72,512]{1,0:T(8,128)(2,1)S(1)} %collective-permute-done.4.refs_0_, bf16[2,256,512]{2,1,0:T(8,128)(2,1)S(1)} %get-tuple-element.13.refs_1_, bf16[2,256,512]{2,1,0:T(8,128)(2,1)S(1)} %get-tuple-element.14.refs_2_, f32[8,256]{1,0:T(8,128)S(1)} %get-tuple-element.15.refs_3_), custom_call_target="tpu_custom_call" | custom-call | bytes 1048576 | tf_op jit(solution)/shard_map/pallas_call | solution.py:282
  10.4 3.8 %collective-permute-start.5 = (bf16[64,512]{1,0:T(8,128)(2,1)S(1)}, bf16[64,512]{1,0:T(8,128)(2,1)S(1)}, u32[]{:S(2)}, u32[]{:S(2)}) collective-permute-start(bf16[64,512]{1,0:T(8,128)(2,1)S(1)} %shard_map.126), channel_id=1, source_target_pairs={{0,12},{4,8},{8,4},{12,0},{1,13},{5,9},{9,5},{13,1},{2,14},{6,10},... | collective-permute-start | bytes 196616 | tf_op jit(solution)/shard_map/ppermute | solution.py:30
  14.2 0.5 %shard_map.124 = bf16[64,512]{1,0:T(8,128)(2,1)S(1)} custom-call(bf16[72,512]{1,0:T(8,128)(2,1)S(1)} %collective-permute-done.refs_0_, bf16[2,256,512]{2,1,0:T(8,128)(2,1)S(1)} %get-tuple-element.13.refs_1_, bf16[2,256,512]{2,1,0:T(8,128)(2,1)S(1)} %get-tuple-element.14.refs_2_, f32[8,256]{1,0:T(8,128)S(1)} %get-tuple-element.15.refs_3_), custom_call_target="tpu_custom_call" | custom-call | bytes 1048576 | tf_op jit(solution)/shard_map/pallas_call | solution.py:282
  14.7 0.1 collective-permute-start.1
  14.8 0.5 %shard_map.125 = bf16[64,512]{1,0:T(8,128)(2,1)S(1)} custom-call(bf16[72,512]{1,0:T(8,128)(2,1)S(1)} %collective-permute-done.2.refs_0_, bf16[2,256,512]{2,1,0:T(8,128)(2,1)S(1)} %get-tuple-element.13.refs_1_, bf16[2,256,512]{2,1,0:T(8,128)(2,1)S(1)} %get-tuple-element.14.refs_2_, f32[8,256]{1,0:T(8,128)S(1)} %get-tuple-element.15.refs_3_), custom_call_target="tpu_custom_call" | custom-call | bytes 1048576 | tf_op jit(solution)/shard_map/pallas_call | solution.py:282
  15.3 0.8 %collective-permute-start.3 = (bf16[64,512]{1,0:T(8,128)(2,1)S(1)}, bf16[64,512]{1,0:T(8,128)(2,1)S(1)}, u32[]{:S(2)}, u32[]{:S(2)}) collective-permute-start(bf16[64,512]{1,0:T(8,128)(2,1)S(1)} %shard_map.125), channel_id=1, source_target_pairs={{0,8},{4,12},{8,0},{12,4},{1,9},{5,13},{9,1},{13,5},{2,10},{6,14},... | collective-permute-start | bytes 196616 | tf_op jit(solution)/shard_map/ppermute | solution.py:30
  16.1 0.6 %collective-permute-done.5.refs_3_ = bf16[64,512]{1,0:T(8,128)(2,1)S(1)} collective-permute-done((bf16[64,512]{1,0:T(8,128)(2,1)S(1)}, bf16[64,512]{1,0:T(8,128)(2,1)S(1)}, u32[]{:S(2)}, u32[]{:S(2)}) %collective-permute-start.5) | collective-permute-done | bytes 65568 | tf_op jit(solution)/shard_map/ppermute | solution.py:30
  16.7 1.5 %collective-permute-start.9 = (bf16[64,512]{1,0:T(8,128)(2,1)S(1)}, bf16[64,512]{1,0:T(8,128)(2,1)S(1)}, u32[]{:S(2)}, u32[]{:S(2)}) collective-permute-start(bf16[64,512]{1,0:T(8,128)(2,1)S(1)} %copy-done.1), channel_id=1, source_target_pairs={{2,0},{0,2},{3,1},{1,3},{6,4},{4,6},{7,5},{5,7},{10,8},{8,10},{11,... | collective-permute-start | bytes 196616 | tf_op jit(solution)/shard_map/ppermute | solution.py:26
  18.2 1.1 %collective-permute-done.1.refs_1_ = bf16[64,512]{1,0:T(8,128)(2,1)S(1)} collective-permute-done((bf16[64,512]{1,0:T(8,128)(2,1)S(1)}, bf16[64,512]{1,0:T(8,128)(2,1)S(1)}, u32[]{:S(2)}, u32[]{:S(2)}) %collective-permute-start.1) | collective-permute-done | bytes 65568 | tf_op jit(solution)/shard_map/ppermute | solution.py:30
  19.3 1.2 %collective-permute-done.3.refs_2_ = bf16[64,512]{1,0:T(8,128)(2,1)S(1)} collective-permute-done((bf16[64,512]{1,0:T(8,128)(2,1)S(1)}, bf16[64,512]{1,0:T(8,128)(2,1)S(1)}, u32[]{:S(2)}, u32[]{:S(2)}) %collective-permute-start.3) | collective-permute-done | bytes 65568 | tf_op jit(solution)/shard_map/ppermute | solution.py:30
  20.6 1.6 %collective-permute-start.6 = (bf16[64,512]{1,0:T(8,128)(2,1)S(1)}, bf16[64,512]{1,0:T(8,128)(2,1)S(1)}, u32[]{:S(2)}, u32[]{:S(2)}) collective-permute-start(bf16[64,512]{1,0:T(8,128)(2,1)S(1)} %get-tuple-element.17), channel_id=1, source_target_pairs={{2,0},{0,2},{3,1},{1,3},{6,4},{4,6},{7,5},{5,7},{10,8},{8,10},{11,... | collective-permute-start | bytes 196616 | tf_op jit(solution)/shard_map/ppermute | solution.py:26
  22.2 0.5 %collective-permute-start.7 = (bf16[64,512]{1,0:T(8,128)(2,1)S(1)}, bf16[64,512]{1,0:T(8,128)(2,1)S(1)}, u32[]{:S(2)}, u32[]{:S(2)}) collective-permute-start(bf16[64,512]{1,0:T(8,128)(2,1)S(1)} %get-tuple-element.17), channel_id=1, source_target_pairs={{1,0},{0,1},{3,2},{2,3},{5,4},{4,5},{7,6},{6,7},{9,8},{8,9},{11,10... | collective-permute-start | bytes 196616 | tf_op jit(solution)/shard_map/ppermute | solution.py:26
  22.7 2.3 %collective-permute-done.6.refs_1_ = bf16[64,512]{1,0:T(8,128)(2,1)S(1)} collective-permute-done((bf16[64,512]{1,0:T(8,128)(2,1)S(1)}, bf16[64,512]{1,0:T(8,128)(2,1)S(1)}, u32[]{:S(2)}, u32[]{:S(2)}) %collective-permute-start.6) | collective-permute-done | bytes 65568 | tf_op jit(solution)/shard_map/ppermute | solution.py:26
  24.9 1.2 %collective-permute-done.8.refs_3_ = bf16[64,512]{1,0:T(8,128)(2,1)S(1)} collective-permute-done((bf16[64,512]{1,0:T(8,128)(2,1)S(1)}, bf16[64,512]{1,0:T(8,128)(2,1)S(1)}, u32[]{:S(2)}, u32[]{:S(2)}) %collective-permute-start.8) | collective-permute-done | bytes 65568 | tf_op jit(solution)/shard_map/ppermute | solution.py:26
  26.2 1.4 %shard_map.128 = (bf16[64,512]{1,0:T(8,128)(2,1)}, f32[1,64]{1,0:T(1,128)S(1)}, f32[1,64]{1,0:T(1,128)S(1)}) custom-call(f32[64,512]{1,0:T(8,128)S(1)} %get-tuple-element.16.refs_0_, bf16[64,512]{1,0:T(8,128)(2,1)S(1)} %collective-permute-done.6.refs_1_, bf16[64,512]{1,0:T(8,128)(2,1)S(1)} %collective-permute-done.7.refs_2_, ...), custom_call_target="tpu_custom_call" | custom-call | flops 536870912 | bytes 4194304 | tf_op jit(solution)/shard_map/pallas_call | solution.py:314
  27.6 1.6 %collective-permute-start.13 = (f32[1,64]{1,0:T(1,128)S(1)}, f32[1,64]{1,0:T(1,128)S(1)}, u32[]{:S(2)}, u32[]{:S(2)}) collective-permute-start(f32[1,64]{1,0:T(1,128)S(1)} %get-tuple-element.21), channel_id=1, source_target_pairs={{0,2},{2,0},{1,3},{3,1},{4,6},{6,4},{5,7},{7,5},{8,10},{10,8},{9,1... | collective-permute-start | bytes 776 | tf_op jit(solution)/shard_map/ppermute | solution.py:30
  29.1 2.0 %collective-permute-done.13 = f32[1,64]{1,0:T(1,128)S(1)} collective-permute-done((f32[1,64]{1,0:T(1,128)S(1)}, f32[1,64]{1,0:T(1,128)S(1)}, u32[]{:S(2)}, u32[]{:S(2)}) %collective-permute-start.13) | collective-permute-done | bytes 288 | tf_op jit(solution)/shard_map/ppermute | solution.py:30
  31.2 0.5 %add_bitcast_fusion = f32[64]{0:T(128)} fusion(f32[1,64]{1,0:T(1,128)S(1)} %get-tuple-element.20, f32[1,64]{1,0:T(1,128)S(1)} %collective-permute-done.13), kind=kLoop, calls=%fused_computation | loop fusion | flops 64 | bytes 768 | tf_op jit(solution)/shard_map/reshape | solution.py:327
  (20 shorter events, 0.1 us)
Async XLA Ops:
  0.6 25.6 %collective-permute-start.12 = (bf16[512,2048]{1,0:T(8,128)(2,1)}, bf16[512,2048]{1,0:T(8,128)(2,1)S(1)}, u32[]{:S(2)}, u32[]{:S(2)}) collective-permute-start(bf16[512,2048]{1,0:T(8,128)(2,1)} %refs_8_.1), channel_id=1, source_target_pairs={{1,0},{0,1},{3,2},{2,3},{5,4},{4,5},{7,6},{6,7},{9,8},{8,9},{11,10... | collective-permute-start | bytes 6291464 | tf_op jit(solution)/shard_map/ppermute | solution.py:26
  2.0 7.8 %collective-permute-start.4 = (bf16[72,512]{1,0:T(8,128)(2,1)S(1)}, bf16[72,512]{1,0:T(8,128)(2,1)S(1)}, u32[]{:S(2)}, u32[]{:S(2)}) collective-permute-start(bf16[72,512]{1,0:T(8,128)(2,1)S(1)} %shard_map.122.packed_ref), channel_id=1, source_target_pairs={{12,0},{8,4},{4,8},{0,12},{13,1},{9,5},{5,9},{1,13},{14,2},{10,6},... | collective-permute-start | bytes 221192 | tf_op jit(solution)/shard_map/ppermute | solution.py:26
  6.7 7.5 %collective-permute-start = (bf16[72,512]{1,0:T(8,128)(2,1)S(1)}, bf16[72,512]{1,0:T(8,128)(2,1)S(1)}, u32[]{:S(2)}, u32[]{:S(2)}) collective-permute-start(bf16[72,512]{1,0:T(8,128)(2,1)S(1)} %shard_map.122.packed_ref), channel_id=1, source_target_pairs={{4,0},{0,4},{12,8},{8,12},{5,1},{1,5},{13,9},{9,13},{6,2},{2,6},{1... | collective-permute-start | bytes 221192 | tf_op jit(solution)/shard_map/ppermute | solution.py:26
  6.7 8.1 %collective-permute-start.2 = (bf16[72,512]{1,0:T(8,128)(2,1)S(1)}, bf16[72,512]{1,0:T(8,128)(2,1)S(1)}, u32[]{:S(2)}, u32[]{:S(2)}) collective-permute-start(bf16[72,512]{1,0:T(8,128)(2,1)S(1)} %shard_map.122.packed_ref), channel_id=1, source_target_pairs={{8,0},{12,4},{0,8},{4,12},{9,1},{13,5},{1,9},{5,13},{10,2},{14,6},... | collective-permute-start | bytes 221192 | tf_op jit(solution)/shard_map/ppermute | solution.py:26
  7.3 9.4 %copy-start.1 = (bf16[64,512]{1,0:T(8,128)(2,1)S(1)}, bf16[64,512]{1,0:T(8,128)(2,1)}, u32[]{:S(2)}) copy-start(bf16[64,512]{1,0:T(8,128)(2,1)} %refs_4_) | copy-start | bytes 196612
  9.2 17.0 %copy-start = (bf16[512,2048]{1,0:T(8,128)(2,1)S(1)}, bf16[512,2048]{1,0:T(8,128)(2,1)}, u32[]{:S(2)}) copy-start(bf16[512,2048]{1,0:T(8,128)(2,1)} %refs_8_.1) | copy-start | bytes 6291460
  9.2 17.0 %copy-start.2 = (f32[2048]{0:T(1024)S(1)}, f32[2048]{0:T(1024)}, u32[]{:S(2)}) copy-start(f32[2048]{0:T(1024)} %param.20) | copy-start | bytes 24580
  9.2 17.0 %copy-start.3 = (f32[2048]{0:T(1024)S(1)}, f32[2048]{0:T(1024)}, u32[]{:S(2)}) copy-start(f32[2048]{0:T(1024)} %param.21) | copy-start | bytes 24580
  10.4 6.3 %collective-permute-start.5 = (bf16[64,512]{1,0:T(8,128)(2,1)S(1)}, bf16[64,512]{1,0:T(8,128)(2,1)S(1)}, u32[]{:S(2)}, u32[]{:S(2)}) collective-permute-start(bf16[64,512]{1,0:T(8,128)(2,1)S(1)} %shard_map.126), channel_id=1, source_target_pairs={{0,12},{4,8},{8,4},{12,0},{1,13},{5,9},{9,5},{13,1},{2,14},{6,10},... | collective-permute-start | bytes 196616 | tf_op jit(solution)/shard_map/ppermute | solution.py:30
  14.7 4.6 %collective-permute-start.1 = (bf16[64,512]{1,0:T(8,128)(2,1)S(1)}, bf16[64,512]{1,0:T(8,128)(2,1)S(1)}, u32[]{:S(2)}, u32[]{:S(2)}) collective-permute-start(bf16[64,512]{1,0:T(8,128)(2,1)S(1)} %shard_map.124), channel_id=1, source_target_pairs={{0,4},{4,0},{8,12},{12,8},{1,5},{5,1},{9,13},{13,9},{2,6},{6,2},{1... | collective-permute-start | bytes 196616 | tf_op jit(solution)/shard_map/ppermute | solution.py:30
  15.3 5.2 %collective-permute-start.3 = (bf16[64,512]{1,0:T(8,128)(2,1)S(1)}, bf16[64,512]{1,0:T(8,128)(2,1)S(1)}, u32[]{:S(2)}, u32[]{:S(2)}) collective-permute-start(bf16[64,512]{1,0:T(8,128)(2,1)S(1)} %shard_map.125), channel_id=1, source_target_pairs={{0,8},{4,12},{8,0},{12,4},{1,9},{5,13},{9,1},{13,5},{2,10},{6,14},... | collective-permute-start | bytes 196616 | tf_op jit(solution)/shard_map/ppermute | solution.py:30
  16.7 5.9 %collective-permute-start.9 = (bf16[64,512]{1,0:T(8,128)(2,1)S(1)}, bf16[64,512]{1,0:T(8,128)(2,1)S(1)}, u32[]{:S(2)}, u32[]{:S(2)}) collective-permute-start(bf16[64,512]{1,0:T(8,128)(2,1)S(1)} %copy-done.1), channel_id=1, source_target_pairs={{2,0},{0,2},{3,1},{1,3},{6,4},{4,6},{7,5},{5,7},{10,8},{8,10},{11,... | collective-permute-start | bytes 196616 | tf_op jit(solution)/shard_map/ppermute | solution.py:26
  20.6 4.3 %collective-permute-start.6 = (bf16[64,512]{1,0:T(8,128)(2,1)S(1)}, bf16[64,512]{1,0:T(8,128)(2,1)S(1)}, u32[]{:S(2)}, u32[]{:S(2)}) collective-permute-start(bf16[64,512]{1,0:T(8,128)(2,1)S(1)} %get-tuple-element.17), channel_id=1, source_target_pairs={{2,0},{0,2},{3,1},{1,3},{6,4},{4,6},{7,5},{5,7},{10,8},{8,10},{11,... | collective-permute-start | bytes 196616 | tf_op jit(solution)/shard_map/ppermute | solution.py:26
  22.1 2.8 %collective-permute-start.10 = (bf16[64,512]{1,0:T(8,128)(2,1)S(1)}, bf16[64,512]{1,0:T(8,128)(2,1)S(1)}, u32[]{:S(2)}, u32[]{:S(2)}) collective-permute-start(bf16[64,512]{1,0:T(8,128)(2,1)S(1)} %copy-done.1), channel_id=1, source_target_pairs={{1,0},{0,1},{3,2},{2,3},{5,4},{4,5},{7,6},{6,7},{9,8},{8,9},{11,10... | collective-permute-start | bytes 196616 | tf_op jit(solution)/shard_map/ppermute | solution.py:26
  22.2 2.8 %collective-permute-start.7 = (bf16[64,512]{1,0:T(8,128)(2,1)S(1)}, bf16[64,512]{1,0:T(8,128)(2,1)S(1)}, u32[]{:S(2)}, u32[]{:S(2)}) collective-permute-start(bf16[64,512]{1,0:T(8,128)(2,1)S(1)} %get-tuple-element.17), channel_id=1, source_target_pairs={{1,0},{0,1},{3,2},{2,3},{5,4},{4,5},{7,6},{6,7},{9,8},{8,9},{11,10... | collective-permute-start | bytes 196616 | tf_op jit(solution)/shard_map/ppermute | solution.py:26
  22.7 2.3 %collective-permute-start.11 = (bf16[64,512]{1,0:T(8,128)(2,1)S(1)}, bf16[64,512]{1,0:T(8,128)(2,1)S(1)}, u32[]{:S(2)}, u32[]{:S(2)}) collective-permute-start(bf16[64,512]{1,0:T(8,128)(2,1)S(1)} %collective-permute-done.9.refs_5_), channel_id=1, source_target_pairs={{1,0},{0,1},{3,2},{2,3},{5,4},{4,5},{7,6},{6,7},{9,8},{8,9},{11,10... | collective-permute-start | bytes 196616 | tf_op jit(solution)/shard_map/ppermute | solution.py:26
  24.9 1.3 %collective-permute-start.8 = (bf16[64,512]{1,0:T(8,128)(2,1)S(1)}, bf16[64,512]{1,0:T(8,128)(2,1)S(1)}, u32[]{:S(2)}, u32[]{:S(2)}) collective-permute-start(bf16[64,512]{1,0:T(8,128)(2,1)S(1)} %collective-permute-done.6.refs_1_), channel_id=1, source_target_pairs={{1,0},{0,1},{3,2},{2,3},{5,4},{4,5},{7,6},{6,7},{9,8},{8,9},{11,10... | collective-permute-start | bytes 196616 | tf_op jit(solution)/shard_map/ppermute | solution.py:26
  27.6 3.6 %collective-permute-start.13 = (f32[1,64]{1,0:T(1,128)S(1)}, f32[1,64]{1,0:T(1,128)S(1)}, u32[]{:S(2)}, u32[]{:S(2)}) collective-permute-start(f32[1,64]{1,0:T(1,128)S(1)} %get-tuple-element.21), channel_id=1, source_target_pairs={{0,2},{2,0},{1,3},{3,1},{4,6},{6,4},{5,7},{7,5},{8,10},{10,8},{9,1... | collective-permute-start | bytes 776 | tf_op jit(solution)/shard_map/ppermute | solution.py:30
